TPU v7x, 128 devices: a whole 4x4x4 slice. The times are simulated.
128 devices in a mesh: space: 32 (over z, y, core), orb: 4 (over x).
Axes of the slice: x: 4, y: 4, z: 4, core: 2. Of those that a mesh axis runs over, the one named last changes fastest.
Arguments:
- orbitals: float32 [8, 32768, 256], P('orb', 'space'), may hold values from -6 to 6
- near_source: int32 [32768, 27], P('space'), may hold values from 0 to 32767, as said below
- far_leaf: int32 [32768, 108], P('space'), may hold values from 0 to 32767, as said below
- far_mid: int32 [4096, 108], P('space'), may hold values from 0 to 4095, as said below
- far_top: int32 [512, 108], P('space'), may hold values from 0 to 511, as said below
- leaf_basis: bfloat16 [64, 256], replicated, may hold values from -0.375 to 0.375
- near_table: bfloat16 [27, 256, 256], replicated, may hold values from -0.078125 to 0.078125
- transfer: bfloat16 [8, 64, 64], replicated, may hold values from -0.75 to 0.75
- coupling: bfloat16 [108, 64, 64], replicated, may hold values from -0.078125 to 0.078125
- pair_transfer: bfloat16 [2, 64, 64], replicated, may hold values from -0.75 to 0.75
- coarse_coupling: bfloat16 [4, 64, 64], replicated, may hold values from -0.4375 to 0.4375
Outputs:
- relaxed: float32 [8, 32768, 256], P('orb', 'space')
Inputs may be any that keep to these rules, and one draw needn't show every extreme that they name: `near_source`: with layer(t) = t // 64: every entry of leaf t lies in a layer at most 1 from layer(t); entry 13 is t itself; entry 0 is the leaf at t's transverse position one layer away. `far_leaf`: with layer(t) = t // 64: every entry of box t lies in a layer 2 or 3 away from layer(t); entry 0 is exactly 3 layers away. `far_mid`: with layer(t) = t // 16: every entry of box t lies in a layer 2 or 3 away from layer(t); entry 0 is exactly 3 layers away. `far_top`: with layer(t) = t // 4: every entry of box t lies in a layer 2 or 3 away from layer(t); entry 0 is exactly 3 layers away.
All inputs are finite; a program needn't handle non-finite values.
Results may differ from a plain program's by a relative error of at most 0.012.
Values may be sent and summed in bfloat16 or wider, within the bound.
A program may use at most 192 MiB of HBM per device.

v0:
```python
import jax
import jax.numpy as jnp
from jax import lax
from jax.sharding import PartitionSpec as P

SIDE = 8
relax_step = 0.1


def padded(cells, sides, width):
    for axis, dim in sides:
        count = lax.axis_size(axis)
        ends = count - 1
        head = lax.slice_in_dim(cells, 0, width, axis=dim)
        tail = lax.slice_in_dim(cells, cells.shape[dim] - width, cells.shape[dim], axis=dim)
        cells = jnp.concatenate(
            [
                lax.ppermute(tail, axis, [(i, (i + 1) % count) for i in range(ends)]),
                cells,
                lax.ppermute(head, axis, [((i + 1) % count, i) for i in range(ends)]),
            ],
            axis=dim,
        )
    return cells


def leaf_project(density, leaf_basis):
    return jnp.einsum(
        "olp,rp->lor", density, leaf_basis, preferred_element_type=jnp.float32
    ).astype(jnp.bfloat16)


def octant_up(moments, side_boxes, transfer):
    node_count, orbits, rank_width = moments.shape
    layers = node_count // (side_boxes * side_boxes)
    half_side = side_boxes // 2
    shaped = moments.reshape(layers // 2, 2, half_side, 2, half_side, 2, orbits, rank_width)
    octant_grid = transfer.reshape(2, 2, 2, rank_width, rank_width)
    parents = jnp.einsum(
        "apbqcuos,pqusr->abcor", shaped, octant_grid, preferred_element_type=jnp.float32
    )
    return parents.reshape(-1, orbits, rank_width).astype(jnp.bfloat16)


def octant_down(coeffs, side_boxes, transfer):
    node_count, orbits, rank_width = coeffs.shape
    layers = node_count // (side_boxes * side_boxes)
    shaped = coeffs.reshape(layers, side_boxes, side_boxes, orbits, rank_width)
    octant_grid = transfer.reshape(2, 2, 2, rank_width, rank_width)
    children = jnp.einsum(
        "abcor,pqusr->apbqcuos", shaped, octant_grid, preferred_element_type=jnp.float32
    )
    return children.reshape(-1, orbits, rank_width)


def couple_rows(moments, sources, coupling, scale):
    node_count, orbits, rank_width = moments.shape
    flattened = moments.reshape(node_count, orbits * rank_width)
    identity = jnp.eye(orbits, dtype=coupling.dtype)
    running = None
    for column_start in range(0, sources.shape[1], 27):
        block_coupling = coupling[column_start : column_start + 27]
        widened = jnp.einsum("ab,krs->kasbr", identity, block_coupling).reshape(
            block_coupling.shape[0], orbits * rank_width, orbits * rank_width
        )
        picked = jnp.take(flattened, sources[:, column_start : column_start + 27], axis=0)
        piece_sum = jnp.einsum("lkx,kxy->ly", picked, widened, preferred_element_type=jnp.float32)
        running = piece_sum if running is None else running + piece_sum
    return scale * running.reshape(-1, orbits, rank_width)


def near_sum(density, sources, near_table):
    running = None
    for column_start in range(0, sources.shape[1], 9):
        picked = jnp.take(density, sources[:, column_start : column_start + 9], axis=1)
        piece_sum = jnp.einsum(
            "olkq,kpq->olp",
            picked,
            near_table[column_start : column_start + 9],
            preferred_element_type=jnp.float32,
        )
        running = piece_sum if running is None else running + piece_sum
    return running


def shifted(values, offset):
    node_count = values.shape[0]
    if abs(offset) >= node_count:
        return jnp.zeros_like(values)
    empty = jnp.zeros((abs(offset), values.shape[1], values.shape[2]), values.dtype)
    if offset > 0:
        return jnp.concatenate([values[offset:], empty], axis=0)
    return jnp.concatenate([empty, values[:offset]], axis=0)


def coarse_couple(moments, coarse_coupling, scale):
    node_count = moments.shape[0]
    odd_rows = (jnp.arange(node_count) % 2).astype(jnp.float32)[:, None, None]
    even_rows = 1.0 - odd_rows

    def apply_matrix(which, offset):
        return jnp.einsum(
            "nos,rs->nor",
            shifted(moments, offset),
            coarse_coupling[which],
            preferred_element_type=jnp.float32,
        )

    running = (
        apply_matrix(1, -2)
        + apply_matrix(2, 2)
        + even_rows * apply_matrix(3, 3)
        + odd_rows * apply_matrix(0, -3)
    )
    return scale * running


def coarse_up(moments, pair_transfer):
    node_count, orbits, rank_width = moments.shape
    shaped = moments.reshape(-1, 2, orbits, rank_width)
    return jnp.einsum(
        "apos,psr->aor", shaped, pair_transfer, preferred_element_type=jnp.float32
    ).astype(jnp.bfloat16)


def coarse_down(coeffs, pair_transfer):
    children = jnp.einsum(
        "aor,psr->apos", coeffs, pair_transfer, preferred_element_type=jnp.float32
    )
    return children.reshape(-1, coeffs.shape[1], coeffs.shape[2])


def coarse_tree(cube_moments, coarse_coupling, pair_transfer):
    levels = [cube_moments]
    while levels[-1].shape[0] > 1:
        levels.append(coarse_up(levels[-1], pair_transfer))
    top_level = len(levels) - 1
    coeffs = coarse_couple(levels[top_level], coarse_coupling, 0.5 ** (3 + top_level)).astype(
        jnp.bfloat16
    )
    for depth_level in range(top_level - 1, -1, -1):
        pushed = coarse_down(coeffs, pair_transfer)
        coupled = coarse_couple(levels[depth_level], coarse_coupling, 0.5 ** (3 + depth_level))
        coeffs = (coupled + pushed).astype(jnp.bfloat16)
    return coeffs


def shards(
    orbitals,
    near_source,
    far_leaf,
    far_mid,
    far_top,
    leaf_basis,
    near_table,
    transfer,
    coupling,
    pair_transfer,
    coarse_coupling,
):
    orbits, leaf_count, points = orbitals.shape
    rank_size = leaf_basis.shape[0]
    device = lax.axis_index("space")
    density = (orbitals * orbitals).astype(jnp.bfloat16)
    layer_size = SIDE * SIDE
    reach_leaves = 12 * layer_size
    density_ext = padded(density, (("space", 1),), layer_size)
    near_start = device * leaf_count - layer_size
    local_moments = leaf_project(density, leaf_basis)
    flattened = local_moments.reshape(leaf_count, orbits * rank_size)
    leaf_ext = padded(flattened, (("space", 0),), reach_leaves).reshape(-1, orbits, rank_size)
    near_field = near_sum(density_ext, near_source - near_start, near_table)
    mid_ext = octant_up(leaf_ext, SIDE, transfer)
    top_ext = octant_up(mid_ext, SIDE // 2, transfer)
    top_count = leaf_count // 64
    mid_count = leaf_count // 8
    top_rim = reach_leaves // 64
    mid_rim = reach_leaves // 8
    top_local = top_ext[top_rim : top_rim + top_count]
    cube_local = octant_up(top_local, SIDE // 4, transfer)
    cube_rows = cube_local.shape[0]
    cube_all = lax.all_gather(
        cube_local.reshape(cube_rows, orbits * rank_size), "space", axis=0, tiled=True
    ).reshape(-1, orbits, rank_size)
    cube_coeffs = coarse_tree(cube_all, coarse_coupling, pair_transfer)
    cube_own = lax.dynamic_slice_in_dim(cube_coeffs, device * cube_rows, cube_rows, 0)
    top_coeffs = (
        couple_rows(top_ext, far_top - (device * top_count - top_rim), coupling, 0.25)
        + octant_down(cube_own, SIDE // 8, transfer)
    ).astype(jnp.bfloat16)
    mid_coeffs = (
        couple_rows(mid_ext, far_mid - (device * mid_count - mid_rim), coupling, 0.5)
        + octant_down(top_coeffs, SIDE // 4, transfer)
    ).astype(jnp.bfloat16)
    leaf_coeffs = (
        couple_rows(leaf_ext, far_leaf - (device * leaf_count - reach_leaves), coupling, 1.0)
        + octant_down(mid_coeffs, SIDE // 2, transfer)
    ).astype(jnp.bfloat16)
    far_field = jnp.einsum(
        "lor,rp->olp", leaf_coeffs, leaf_basis, preferred_element_type=jnp.float32
    )
    potential = near_field + far_field
    hartree = lax.psum(jnp.sum(potential, axis=0).astype(jnp.bfloat16), "orb").astype(jnp.float32)
    return orbitals - relax_step * (hartree[None] - potential) * orbitals


def solution(mesh):
    placed = (
        P("orb", "space", None),
        P("space", None),
        P("space", None),
        P("space", None),
        P("space", None),
        P(),
        P(),
        P(),
        P(),
        P(),
        P(),
    )
    return jax.shard_map(
        shards, mesh=mesh, in_specs=placed, out_specs=P("orb", "space", None), check_vma=False
    )
```

profile of v0, /device:TPU:0, one launch (start us, length us, event | category | flops | bytes accessed | tf_op | source)
XLA Modules:
  0.0 1078.0 jit_solution(17902328975907240493)
XLA Ops:
  15.3 4.8 collective-permute-start
  55.0 9.0 multiply_bitcast_fusion
  77.4 4.4 reshape.258
  105.5 7.3 copy.392
  112.7 71.8 %gather_fusion.2 = bf16[9216,2,256]{2,1,0:T(2,128)(2,1)} fusion(bf16[2,1152,256]{2,0,1:T(2,128)(2,1)S(1)} %copy.392, s32[9216]{0:T(1024)S(1)} %broadcast_clamp_fusion.4), kind=kCustom, calls=%fused_computation.5.clone | custom fusion | bytes 18911232 | tf_op jit(solution)/shard_map/jit(_take)/gather | solution.py:75
  184.6 71.8 %gather_fusion.1 = bf16[9216,2,256]{2,1,0:T(2,128)(2,1)} fusion(bf16[2,1152,256]{2,0,1:T(2,128)(2,1)S(1)} %copy.392, s32[9216]{0:T(1024)S(1)} %broadcast_clamp_fusion.5), kind=kCustom, calls=%fused_computation.4.clone | custom fusion | bytes 18911232 | tf_op jit(solution)/shard_map/jit(_take)/gather | solution.py:75
  256.4 71.8 %gather_fusion = bf16[9216,2,256]{2,1,0:T(2,128)(2,1)} fusion(bf16[2,1152,256]{2,0,1:T(2,128)(2,1)S(1)} %copy.392, s32[9216]{0:T(1024)S(1)} %broadcast_clamp_fusion.6), kind=kCustom, calls=%fused_computation.clone | custom fusion | bytes 18911232 | tf_op jit(solution)/shard_map/jit(_take)/gather | solution.py:75
  328.2 18.5 %fusion.2 = bf16[2,1024,9,256]{3,0,2,1:T(2,128)(2,1)S(1)} fusion(bf16[1024,9,2,256]{3,2,1,0:T(2,128)(2,1)} %bitcast.386, pred[1024,9]{1,0:T(8,128)(4,1)S(1)} %copy-done.18), kind=kLoop, calls=%fused_computation.20 | loop fusion | flops 4718592 | bytes 18883584 | tf_op jit(solution)/shard_map/jit(_take)/select_n | solution.py:75
  350.8 16.6 %fusion.1 = bf16[2,1024,9,256]{3,0,2,1:T(2,128)(2,1)S(1)} fusion(bf16[1024,9,2,256]{3,2,1,0:T(2,128)(2,1)S(1)} %bitcast.385, pred[1024,9]{1,0:T(8,128)(4,1)S(1)} %copy-done.19), kind=kLoop, calls=%fused_computation.19 | loop fusion | flops 4718592 | bytes 18883584 | tf_op jit(solution)/shard_map/jit(_take)/select_n | solution.py:75
  367.5 18.0 %fusion = bf16[2,1024,9,256]{3,0,2,1:T(2,128)(2,1)} fusion(bf16[1024,9,2,256]{3,2,1,0:T(2,128)(2,1)S(1)} %bitcast.382, pred[1024,9]{1,0:T(8,128)(4,1)S(1)} %copy-done.20), kind=kLoop, calls=%fused_computation.18 | loop fusion | flops 4718592 | bytes 18883584 | tf_op jit(solution)/shard_map/jit(_take)/select_n | solution.py:75
  395.6 28.1 %all-gather = bf16[32,2,128]{2,1,0:T(2,128)(2,1)S(1)} all-gather(bf16[1,2,128]{2,1,0:T(2,128)(2,1)S(1)} %reshape.425), channel_id=1, replica_groups=mesh['space'=32,'orb'=4] {'space'}, dimensions={0}, use_global_device_ids=true | all-gather | bytes 16896 | tf_op jit(solution)/shard_map/all_gather | solution.py:182
  449.5 8.2 gather_fusion.10
  463.2 7.1 gather_fusion.9
  475.8 7.1 gather_fusion.8
  488.4 7.1 gather_fusion.7
  504.7 96.4 %gather_fusion.3 = bf16[27648,128]{1,0:T(8,128)(2,1)} fusion(bf16[2560,128]{1,0:T(8,128)(2,1)S(1)} %pad_maximum_fusion.1, s32[27648]{0:T(1024)S(1)} %broadcast_clamp_fusion.3), kind=kCustom, calls=%fused_computation.1.clone | custom fusion | bytes 14266368 | tf_op jit(solution)/shard_map/jit(_take)/gather | solution.py:66
  601.1 11.9 %reshape.448 = bf16[1024,27,128]{2,1,0:T(8,128)(2,1)} reshape(bf16[27648,128]{1,0:T(8,128)(2,1)} %gather_fusion.3) | data formatting | bytes 14155776 | tf_op jit(solution)/shard_map/jit(_take)/gather | solution.py:66
  613.1 15.5 %broadcast_select_fusion.6 = bf16[1024,27,128]{2,1,0:T(8,128)(2,1)S(1)} fusion(bf16[1024,27,128]{2,1,0:T(8,128)(2,1)} %reshape.448, pred[1024,27]{1,0:T(8,128)(4,1)S(1)} %copy-done.17), kind=kLoop, calls=%fused_computation.30 | loop fusion | flops 3538944 | bytes 14183424 | tf_op jit(solution)/shard_map/jit(_take)/select_n | solution.py:66
  632.9 96.4 %gather_fusion.4 = bf16[27648,128]{1,0:T(8,128)(2,1)} fusion(bf16[2560,128]{1,0:T(8,128)(2,1)S(1)} %pad_maximum_fusion.1, s32[27648]{0:T(1024)S(1)} %broadcast_clamp_fusion.2), kind=kCustom, calls=%fused_computation.6.clone | custom fusion | bytes 14266368 | tf_op jit(solution)/shard_map/jit(_take)/gather | solution.py:66
  729.3 11.9 %reshape.452 = bf16[1024,27,128]{2,1,0:T(8,128)(2,1)} reshape(bf16[27648,128]{1,0:T(8,128)(2,1)} %gather_fusion.4) | data formatting | bytes 14155776 | tf_op jit(solution)/shard_map/jit(_take)/gather | solution.py:66
  741.2 96.4 %gather_fusion.5 = bf16[27648,128]{1,0:T(8,128)(2,1)} fusion(bf16[2560,128]{1,0:T(8,128)(2,1)S(1)} %pad_maximum_fusion.1, s32[27648]{0:T(1024)S(1)} %broadcast_clamp_fusion.1), kind=kCustom, calls=%fused_computation.7.clone | custom fusion | bytes 14266368 | tf_op jit(solution)/shard_map/jit(_take)/gather | solution.py:66
  837.6 11.9 %reshape.456 = bf16[1024,27,128]{2,1,0:T(8,128)(2,1)} reshape(bf16[27648,128]{1,0:T(8,128)(2,1)} %gather_fusion.5) | data formatting | bytes 14155776 | tf_op jit(solution)/shard_map/jit(_take)/gather | solution.py:66
  849.5 96.4 %gather_fusion.6 = bf16[27648,128]{1,0:T(8,128)(2,1)} fusion(bf16[2560,128]{1,0:T(8,128)(2,1)S(1)} %pad_maximum_fusion.1, s32[27648]{0:T(1024)S(1)} %copy-done.4), kind=kCustom, calls=%fused_computation.8.clone | custom fusion | bytes 14266368 | tf_op jit(solution)/shard_map/jit(_take)/gather | solution.py:66
  945.9 11.9 %reshape.460 = bf16[1024,27,128]{2,1,0:T(8,128)(2,1)} reshape(bf16[27648,128]{1,0:T(8,128)(2,1)} %gather_fusion.6) | data formatting | bytes 14155776 | tf_op jit(solution)/shard_map/jit(_take)/gather | solution.py:66
  957.9 15.4 %broadcast_select_fusion.5 = bf16[1024,27,128]{2,1,0:T(8,128)(2,1)S(1)} fusion(bf16[1024,27,128]{2,1,0:T(8,128)(2,1)} %reshape.452, pred[1024,27]{1,0:T(8,128)(4,1)S(1)} %copy-done.14), kind=kLoop, calls=%fused_computation.29 | loop fusion | flops 3538944 | bytes 14183424 | tf_op jit(solution)/shard_map/jit(_take)/select_n | solution.py:66
  973.3 4.3 fusion.37
  977.7 15.7 %broadcast_select_fusion.4 = bf16[1024,27,128]{2,1,0:T(8,128)(2,1)S(1)} fusion(bf16[1024,27,128]{2,1,0:T(8,128)(2,1)} %reshape.456, pred[1024,27]{1,0:T(8,128)(4,1)S(1)} %copy-done.15), kind=kLoop, calls=%fused_computation.28 | loop fusion | flops 3538944 | bytes 14183424 | tf_op jit(solution)/shard_map/jit(_take)/select_n | solution.py:66
  993.5 4.3 fusion.34
  997.8 13.7 %broadcast_select_fusion.3 = bf16[1024,27,128]{2,1,0:T(8,128)(2,1)S(1)} fusion(bf16[1024,27,128]{2,1,0:T(8,128)(2,1)S(1)} %bitcast.388, pred[1024,27]{1,0:T(8,128)(4,1)S(1)} %copy-done.16), kind=kLoop, calls=%fused_computation.27 | loop fusion | flops 3538944 | bytes 14183424 | tf_op jit(solution)/shard_map/jit(_take)/select_n | solution.py:66
  1011.6 4.3 fusion.31
  1016.5 7.0 fusion.300
  1023.5 43.0 %all-reduce.22.cloned.1.call-done = bf16[1024,256]{1,0:T(8,128)(2,1)} async-done(((bf16[1024,256]{1,0:T(8,128)(2,1)}), bf16[1024,256]{1,0:T(8,128)(2,1)}) %all-reduce.22.cloned.1.call-update) | async-done | bytes 524304 | tf_op jit(solution)/shard_map/psum | solution.py:203
  (335 shorter events, 154.4 us)
Async XLA Ops:
  6.5 387.6 %copy-start = (bf16[8,64,64]{2,1,0:T(8,128)(2,1)S(1)}, bf16[8,64,64]{2,1,0:T(8,128)(2,1)}, u32[]{:S(2)}) copy-start(bf16[8,64,64]{2,1,0:T(8,128)(2,1)} %param.26) | copy-start | bytes 196612
  6.5 29.9 %copy-start.11 = (bf16[4,64,64]{2,1,0:T(8,128)(2,1)S(1)}, bf16[4,64,64]{2,1,0:T(8,128)(2,1)}, u32[]{:S(2)}) copy-start(bf16[4,64,64]{2,1,0:T(8,128)(2,1)} %param.29) | copy-start | bytes 98308
  6.5 25.2 %copy-start.24 = (s32[1024,108]{0,1:T(8,128)S(1)}, s32[1024,108]{0,1:T(8,128)}, u32[]{:S(2)}) copy-start(s32[1024,108]{0,1:T(8,128)} %param.21) | copy-start | bytes 1327108
  6.5 30.7 %copy-start.9 = (bf16[2,64,64]{2,1,0:T(8,128)(2,1)S(1)}, bf16[2,64,64]{2,1,0:T(8,128)(2,1)}, u32[]{:S(2)}) copy-start(bf16[2,64,64]{2,1,0:T(8,128)(2,1)} %param.28) | copy-start | bytes 49156
  6.5 34.3 %copy-start.2 = (bf16[108,64,64]{0,2,1:T(8,128)(2,1)S(1)}, bf16[108,64,64]{0,2,1:T(8,128)(2,1)}, u32[]{:S(2)}) copy-start(bf16[108,64,64]{0,2,1:T(8,128)(2,1)} %param.27) | copy-start | bytes 2654212
  6.5 1059.9 %all-reduce.22.cloned.1.call-start = ((), (), s32[]{:S(2)}) async-start(), calls=%async_computation | async-start | bytes 1048576 | tf_op jit(solution)/shard_map/psum | solution.py:203
  10.5 379.0 %collective-permute-start.2 = (bf16[768,128]{1,0:T(8,128)(2,1)}, bf16[768,128]{1,0:T(8,128)(2,1)}, u32[]{:S(2)}, u32[]{:S(2)}) collective-permute-start(bf16[768,128]{1,0:T(8,128)(2,1)} %copy.403), channel_id=1, source_target_pairs={{0,4},{4,8},{8,12},{12,16},{16,20},{20,24},{24,28},{28,32},{32,36}... | collective-permute-start | bytes 589832 | tf_op jit(solution)/shard_map/ppermute | solution.py:18
  13.3 376.3 %collective-permute-start.3 = (bf16[768,128]{1,0:T(8,128)(2,1)}, bf16[768,128]{1,0:T(8,128)(2,1)}, u32[]{:S(2)}, u32[]{:S(2)}) collective-permute-start(bf16[768,128]{1,0:T(8,128)(2,1)} %copy.404), channel_id=1, source_target_pairs={{4,0},{8,4},{12,8},{16,12},{20,16},{24,20},{28,24},{32,28},{36,32}... | collective-permute-start | bytes 589832 | tf_op jit(solution)/shard_map/ppermute | solution.py:20
  15.3 89.3 %collective-permute-start = (bf16[2,64,256]{2,1,0:T(8,128)(2,1)}, bf16[2,64,256]{2,1,0:T(8,128)(2,1)}, u32[]{:S(2)}, u32[]{:S(2)}) collective-permute-start(bf16[2,64,256]{2,1,0:T(8,128)(2,1)} %get-tuple-element.6), channel_id=1, source_target_pairs={{0,4},{4,8},{8,12},{12,16},{16,20},{20,24},{24,28},{28,32},{32,36}... | collective-permute-start | bytes 196616 | tf_op jit(solution)/shard_map/ppermute | solution.py:18
  20.1 84.4 %collective-permute-start.1 = (bf16[2,64,256]{2,1,0:T(8,128)(2,1)}, bf16[2,64,256]{2,1,0:T(8,128)(2,1)}, u32[]{:S(2)}, u32[]{:S(2)}) collective-permute-start(bf16[2,64,256]{2,1,0:T(8,128)(2,1)} %get-tuple-element.8), channel_id=1, source_target_pairs={{4,0},{8,4},{12,8},{16,12},{20,16},{24,20},{28,24},{32,28},{36,32}... | collective-permute-start | bytes 196616 | tf_op jit(solution)/shard_map/ppermute | solution.py:20
  64.0 19.5 %copy-start.35 = (s32[128,27]{0,1:T(8,128)S(1)}, s32[128,27]{0,1:T(8,128)}, u32[]{:S(2)}) copy-start(s32[128,27]{0,1:T(8,128)} %get-tuple-element.37) | copy-start | bytes 41476
  64.0 20.4 %copy-start.41 = (pred[128,27]{0,1:T(8,128)(4,1)S(1)}, pred[128,27]{0,1:T(8,128)(4,1)}, u32[]{:S(2)}) copy-start(pred[128,27]{0,1:T(8,128)(4,1)} %get-tuple-element.33) | copy-start | bytes 10372
  64.0 25.9 %copy-start.23 = (s32[1024,27]{0,1:T(8,128)S(1)}, s32[1024,27]{0,1:T(8,128)}, u32[]{:S(2)}) copy-start(s32[1024,27]{0,1:T(8,128)} %get-tuple-element.21) | copy-start | bytes 331780
  64.0 27.3 %copy-start.22 = (s32[1024,27]{0,1:T(8,128)S(1)}, s32[1024,27]{0,1:T(8,128)}, u32[]{:S(2)}) copy-start(s32[1024,27]{0,1:T(8,128)} %get-tuple-element.20) | copy-start | bytes 331780
  67.5 26.1 %copy-start.21 = (s32[1024,27]{0,1:T(8,128)S(1)}, s32[1024,27]{0,1:T(8,128)}, u32[]{:S(2)}) copy-start(s32[1024,27]{0,1:T(8,128)} %get-tuple-element.19) | copy-start | bytes 331780
  73.2 26.3 %copy-start.29 = (s32[1024,9]{0,1:T(8,128)S(1)}, s32[1024,9]{0,1:T(8,128)}, u32[]{:S(2)}) copy-start(s32[1024,9]{0,1:T(8,128)} %get-tuple-element.30) | copy-start | bytes 110596
  77.4 24.3 %copy-start.28 = (s32[1024,9]{0,1:T(8,128)S(1)}, s32[1024,9]{0,1:T(8,128)}, u32[]{:S(2)}) copy-start(s32[1024,9]{0,1:T(8,128)} %get-tuple-element.28) | copy-start | bytes 110596
  256.4 71.8 %copy-start.18 = (pred[1024,9]{1,0:T(8,128)(4,1)S(1)}, pred[1024,9]{1,0:T(8,128)(4,1)}, u32[]{:S(2)}) copy-start(pred[1024,9]{1,0:T(8,128)(4,1)} %copy.398) | copy-start | bytes 27652
  328.2 22.5 %slice-start.3 = ((s8[9437184]{0:T(1024)(128)(4,1)}), s8[4194304]{0:T(1024)(128)(4,1)S(1)}, s32[]{:S(2)}) async-start(s8[9437184]{0:T(1024)(128)(4,1)} %bitcast.383), calls=%async_computation.4 | async-start | bytes 8388608
  328.2 22.5 %slice-start.4 = ((s8[9437184]{0:T(1024)(128)(4,1)}), s8[4194304]{0:T(1024)(128)(4,1)S(1)}, s32[]{:S(2)}) async-start(s8[9437184]{0:T(1024)(128)(4,1)} %bitcast.383), calls=%async_computation.5 | async-start | bytes 8388608
  346.7 20.7 %slice-start = ((s8[9437184]{0:T(1024)(128)(4,1)}), s8[4194304]{0:T(1024)(128)(4,1)S(1)}, s32[]{:S(2)}) async-start(s8[9437184]{0:T(1024)(128)(4,1)} %bitcast.380), calls=%async_computation.1 | async-start | bytes 8388608
  346.7 20.7 %slice-start.1 = ((s8[9437184]{0:T(1024)(128)(4,1)}), s8[1048576]{0:T(1024)(128)(4,1)S(1)}, s32[]{:S(2)}) async-start(s8[9437184]{0:T(1024)(128)(4,1)} %bitcast.380), calls=%async_computation.2 | async-start | bytes 2097152
  389.5 34.2 %copy-start.10 = (bf16[2,64,64]{2,1,0:T(8,128)(2,1)S(1)}, bf16[2,64,64]{2,1,0:T(8,128)(2,1)}, u32[]{:S(2)}) copy-start(bf16[2,64,64]{2,1,0:T(8,128)(2,1)} %param.28) | copy-start | bytes 49156
  389.5 35.2 %copy-start.12 = (bf16[4,64,64]{2,1,0:T(8,128)(2,1)S(1)}, bf16[4,64,64]{2,1,0:T(8,128)(2,1)}, u32[]{:S(2)}) copy-start(bf16[4,64,64]{2,1,0:T(8,128)(2,1)} %param.29) | copy-start | bytes 98308
  389.5 47.4 %copy-start.37 = (s32[1024]{0:T(1024)S(1)}, s32[1024]{0:T(1024)}, u32[]{:S(2)}) copy-start(s32[1024]{0:T(1024)} %pad_clamp_fusion.7) | copy-start | bytes 12292
  389.5 49.0 %copy-start.38 = (s32[1024]{0:T(1024)S(1)}, s32[1024]{0:T(1024)}, u32[]{:S(2)}) copy-start(s32[1024]{0:T(1024)} %pad_clamp_fusion.6) | copy-start | bytes 12292
  389.6 51.2 %copy-start.39 = (s32[1024]{0:T(1024)S(1)}, s32[1024]{0:T(1024)}, u32[]{:S(2)}) copy-start(s32[1024]{0:T(1024)} %pad_clamp_fusion.5) | copy-start | bytes 12292
  394.7 54.3 %copy-start.6 = (bf16[27,128,128]{2,1,0:T(8,128)(2,1)S(1)}, bf16[27,128,128]{2,1,0:T(8,128)(2,1)}, u32[]{:S(2)}) copy-start(bf16[27,128,128]{2,1,0:T(8,128)(2,1)} %reshape.258) | copy-start | bytes 2654212
  973.3 24.5 %slice-start.6 = ((s8[8388608]{0:T(1024)(128)(4,1)}), s8[4194304]{0:T(1024)(128)(4,1)S(1)}, s32[]{:S(2)}) async-start(s8[8388608]{0:T(1024)(128)(4,1)} %bitcast.387), calls=%async_computation.7 | async-start | bytes 8388608
  977.7 20.1 %slice-start.7 = ((s8[8388608]{0:T(1024)(128)(4,1)}), s8[4194304]{0:T(1024)(128)(4,1)S(1)}, s32[]{:S(2)}) async-start(s8[8388608]{0:T(1024)(128)(4,1)} %bitcast.387), calls=%async_computation.8 | async-start | bytes 8388608
  1016.5 51.1 %copy-start.3 = (f32[2,1024,256]{2,1,0:T(8,128)S(1)}, f32[2,1024,256]{2,1,0:T(8,128)}, u32[]{:S(2)}) copy-start(f32[2,1024,256]{2,1,0:T(8,128)} %param.19) | copy-start | bytes 6291460
  1016.5 54.3 %copy-start.1 = (bf16[8,64,64]{2,1,0:T(8,128)(2,1)S(1)}, bf16[8,64,64]{2,1,0:T(8,128)(2,1)}, u32[]{:S(2)}) copy-start(bf16[8,64,64]{2,1,0:T(8,128)(2,1)} %param.26) | copy-start | bytes 196612
  (31 other events, 372.2 us)
Sparse Core Ops, SparseCore 0:
  1023.6 42.8 all-reduce.21
where the time goes:
time: 1090 us; the launch traced here: 1080 us
  local copies, waits for them, and re-layouts  761 us (70%)
  other arithmetic  162 us (15%)
  matrix products  58.8 us (5%)
  waiting for transfers between devices  43 us (4%)
  blocking collectives  28.1 us (3%)
  between operations  15 us (1%)
    gather x24, local copies, waits for them, and re-layouts, couple_rows(): jnp.take(flattened, sources[:, column_start:column_start + 27], axis=0)  475 us
    gather x3, local copies, waits for them, and re-layouts, near_sum(): jnp.take(density, sources[:, column_start:column_start + 9], axis=1)  215 us
    select_n x13, other arithmetic, couple_rows(): jnp.take(flattened, sources[:, column_start:column_start + 27], axis=0)  74.5 us
    select_n x4, other arithmetic, near_sum(): jnp.take(density, sources[:, column_start:column_start + 9], axis=1)  53.8 us
    psum x1, waiting for transfers between devices, shards(): lax.psum(jnp.sum(potential, axis=0).astype(jnp.bfloat16), 'orb')  43 us
    all_gather x1, blocking collectives, shards(): lax.all_gather(cube_local.reshape(cube_rows, orbits * rank_size), 'space'...  28.1 us
    dot_general x12, matrix products, couple_rows(): jnp.einsum('lkx,kxy->ly', picked, widened, preferred_element_type=jnp.flo...  26 us
  transfers between devices with their start and end apart: 5, of which 1 were waited for; matrix products, arithmetic and copies ran while one was open for 34% of the time, Pallas kernels for 0%

commit v1 on v0

--- a/solution.py
+++ b/solution.py
@@ -200,7 +200,9 @@
         "lor,rp->olp", leaf_coeffs, leaf_basis, preferred_element_type=jnp.float32
     )
     potential = near_field + far_field
-    hartree = lax.psum(jnp.sum(potential, axis=0).astype(jnp.bfloat16), "orb").astype(jnp.float32)
+    hartree = jnp.sum(
+        lax.all_gather(jnp.sum(potential, axis=0).astype(jnp.bfloat16), "orb"), axis=0
+    ).astype(jnp.float32)
     return orbitals - relax_step * (hartree[None] - potential) * orbitals
 
 

time: 1090 us -> 1080 us (level)
  waiting for transfers between devices: 43 us -> 30.9 us
    psum x1 -> x0, waiting for transfers between devices: 43 us -> none  [shards(): lax.psum(jnp.sum(potential, axis=0).astype(jnp.bfloat16), 'orb')]
    all_gather x0 -> x1, waiting for transfers between devices: none -> 30.8 us  [shards(): lax.all_gather(jnp.sum(potential, axis=0).astype(jnp.bfloat16), 'orb')]
  transfers between devices with their start and end apart: 5 -> 5, of which waited for: 1 -> 1; matrix products, arithmetic and copies ran while one was open for 34% -> 35% of each run, Pallas kernels for 0% -> 0%
where the time goes in v1:
time: 1080 us; the launch traced here: 1070 us
  local copies, waits for them, and re-layouts  761 us (70%)
  other arithmetic  164 us (15%)
  matrix products  58.8 us (5%)
  waiting for transfers between devices  30.9 us (3%)
  blocking collectives  28.1 us (3%)
  between operations  15 us (1%)
    gather x24, local copies, waits for them, and re-layouts, couple_rows(): jnp.take(flattened, sources[:, column_start:column_start + 27], axis=0)  475 us
    gather x3, local copies, waits for them, and re-layouts, near_sum(): jnp.take(density, sources[:, column_start:column_start + 9], axis=1)  215 us
    select_n x13, other arithmetic, couple_rows(): jnp.take(flattened, sources[:, column_start:column_start + 27], axis=0)  74.5 us
    select_n x4, other arithmetic, near_sum(): jnp.take(density, sources[:, column_start:column_start + 9], axis=1)  53.8 us
    all_gather x1, waiting for transfers between devices, shards(): lax.all_gather(jnp.sum(potential, axis=0).astype(jnp.bfloat16), 'orb')  30.8 us
    all_gather x1, blocking collectives, shards(): lax.all_gather(cube_local.reshape(cube_rows, orbits * rank_size), 'space'...  28.1 us
    dot_general x12, matrix products, couple_rows(): jnp.einsum('lkx,kxy->ly', picked, widened, preferred_element_type=jnp.flo...  26 us
  transfers between devices with their start and end apart: 5, of which 1 were waited for; matrix products, arithmetic and copies ran while one was open for 35% of the time, Pallas kernels for 0%

profile of v1, /device:TPU:0, one launch (start us, length us, event | category | flops | bytes accessed | tf_op | source)
XLA Modules:
  0.0 1067.0 jit_solution(1161571349483743047)
XLA Ops:
  15.3 4.8 collective-permute-start
  55.0 9.0 multiply_bitcast_fusion
  77.4 4.4 reshape.268
  105.5 7.3 copy.476
  112.7 71.8 %gather_fusion.2 = bf16[9216,2,256]{2,1,0:T(2,128)(2,1)} fusion(bf16[2,1152,256]{2,0,1:T(2,128)(2,1)S(1)} %copy.476, s32[9216]{0:T(1024)S(1)} %broadcast_clamp_fusion.4), kind=kCustom, calls=%fused_computation.5.clone | custom fusion | bytes 18911232 | tf_op jit(solution)/shard_map/jit(_take)/gather | solution.py:75
  184.6 71.8 %gather_fusion.1 = bf16[9216,2,256]{2,1,0:T(2,128)(2,1)} fusion(bf16[2,1152,256]{2,0,1:T(2,128)(2,1)S(1)} %copy.476, s32[9216]{0:T(1024)S(1)} %broadcast_clamp_fusion.5), kind=kCustom, calls=%fused_computation.4.clone | custom fusion | bytes 18911232 | tf_op jit(solution)/shard_map/jit(_take)/gather | solution.py:75
  256.4 71.8 %gather_fusion = bf16[9216,2,256]{2,1,0:T(2,128)(2,1)} fusion(bf16[2,1152,256]{2,0,1:T(2,128)(2,1)S(1)} %copy.476, s32[9216]{0:T(1024)S(1)} %broadcast_clamp_fusion.6), kind=kCustom, calls=%fused_computation.clone | custom fusion | bytes 18911232 | tf_op jit(solution)/shard_map/jit(_take)/gather | solution.py:75
  328.2 18.5 %fusion.2 = bf16[2,1024,9,256]{3,0,2,1:T(2,128)(2,1)S(1)} fusion(bf16[1024,9,2,256]{3,2,1,0:T(2,128)(2,1)} %bitcast.387, pred[1024,9]{1,0:T(8,128)(4,1)S(1)} %copy-done.18), kind=kLoop, calls=%fused_computation.20 | loop fusion | flops 4718592 | bytes 18883584 | tf_op jit(solution)/shard_map/jit(_take)/select_n | solution.py:75
  350.8 16.6 %fusion.1 = bf16[2,1024,9,256]{3,0,2,1:T(2,128)(2,1)S(1)} fusion(bf16[1024,9,2,256]{3,2,1,0:T(2,128)(2,1)S(1)} %bitcast.386, pred[1024,9]{1,0:T(8,128)(4,1)S(1)} %copy-done.19), kind=kLoop, calls=%fused_computation.19 | loop fusion | flops 4718592 | bytes 18883584 | tf_op jit(solution)/shard_map/jit(_take)/select_n | solution.py:75
  367.5 18.0 %fusion = bf16[2,1024,9,256]{3,0,2,1:T(2,128)(2,1)} fusion(bf16[1024,9,2,256]{3,2,1,0:T(2,128)(2,1)S(1)} %bitcast.383, pred[1024,9]{1,0:T(8,128)(4,1)S(1)} %copy-done.20), kind=kLoop, calls=%fused_computation.18 | loop fusion | flops 4718592 | bytes 18883584 | tf_op jit(solution)/shard_map/jit(_take)/select_n | solution.py:75
  395.6 28.1 %all-gather.1 = bf16[32,2,128]{2,1,0:T(2,128)(2,1)S(1)} all-gather(bf16[1,2,128]{2,1,0:T(2,128)(2,1)S(1)} %reshape.436), channel_id=1, replica_groups=mesh['space'=32,'orb'=4] {'space'}, dimensions={0}, use_global_device_ids=true | all-gather | bytes 16896 | tf_op jit(solution)/shard_map/all_gather | solution.py:182
  449.5 8.2 gather_fusion.10
  463.2 7.1 gather_fusion.9
  475.8 7.1 gather_fusion.8
  488.4 7.1 gather_fusion.7
  504.7 96.4 %gather_fusion.3 = bf16[27648,128]{1,0:T(8,128)(2,1)} fusion(bf16[2560,128]{1,0:T(8,128)(2,1)S(1)} %pad_maximum_fusion.1, s32[27648]{0:T(1024)S(1)} %broadcast_clamp_fusion.3), kind=kCustom, calls=%fused_computation.1.clone | custom fusion | bytes 14266368 | tf_op jit(solution)/shard_map/jit(_take)/gather | solution.py:66
  601.1 11.9 %reshape.459 = bf16[1024,27,128]{2,1,0:T(8,128)(2,1)} reshape(bf16[27648,128]{1,0:T(8,128)(2,1)} %gather_fusion.3) | data formatting | bytes 14155776 | tf_op jit(solution)/shard_map/jit(_take)/gather | solution.py:66
  613.1 15.5 %broadcast_select_fusion.6 = bf16[1024,27,128]{2,1,0:T(8,128)(2,1)S(1)} fusion(bf16[1024,27,128]{2,1,0:T(8,128)(2,1)} %reshape.459, pred[1024,27]{1,0:T(8,128)(4,1)S(1)} %copy-done.17), kind=kLoop, calls=%fused_computation.30 | loop fusion | flops 3538944 | bytes 14183424 | tf_op jit(solution)/shard_map/jit(_take)/select_n | solution.py:66
  632.9 96.4 %gather_fusion.4 = bf16[27648,128]{1,0:T(8,128)(2,1)} fusion(bf16[2560,128]{1,0:T(8,128)(2,1)S(1)} %pad_maximum_fusion.1, s32[27648]{0:T(1024)S(1)} %broadcast_clamp_fusion.2), kind=kCustom, calls=%fused_computation.6.clone | custom fusion | bytes 14266368 | tf_op jit(solution)/shard_map/jit(_take)/gather | solution.py:66
  729.3 11.9 %reshape.463 = bf16[1024,27,128]{2,1,0:T(8,128)(2,1)} reshape(bf16[27648,128]{1,0:T(8,128)(2,1)} %gather_fusion.4) | data formatting | bytes 14155776 | tf_op jit(solution)/shard_map/jit(_take)/gather | solution.py:66
  741.2 96.4 %gather_fusion.5 = bf16[27648,128]{1,0:T(8,128)(2,1)} fusion(bf16[2560,128]{1,0:T(8,128)(2,1)S(1)} %pad_maximum_fusion.1, s32[27648]{0:T(1024)S(1)} %broadcast_clamp_fusion.1), kind=kCustom, calls=%fused_computation.7.clone | custom fusion | bytes 14266368 | tf_op jit(solution)/shard_map/jit(_take)/gather | solution.py:66
  837.6 11.9 %reshape.467 = bf16[1024,27,128]{2,1,0:T(8,128)(2,1)} reshape(bf16[27648,128]{1,0:T(8,128)(2,1)} %gather_fusion.5) | data formatting | bytes 14155776 | tf_op jit(solution)/shard_map/jit(_take)/gather | solution.py:66
  849.5 96.4 %gather_fusion.6 = bf16[27648,128]{1,0:T(8,128)(2,1)} fusion(bf16[2560,128]{1,0:T(8,128)(2,1)S(1)} %pad_maximum_fusion.1, s32[27648]{0:T(1024)S(1)} %copy-done.4), kind=kCustom, calls=%fused_computation.8.clone | custom fusion | bytes 14266368 | tf_op jit(solution)/shard_map/jit(_take)/gather | solution.py:66
  945.9 11.9 %reshape.471 = bf16[1024,27,128]{2,1,0:T(8,128)(2,1)} reshape(bf16[27648,128]{1,0:T(8,128)(2,1)} %gather_fusion.6) | data formatting | bytes 14155776 | tf_op jit(solution)/shard_map/jit(_take)/gather | solution.py:66
  957.9 15.4 %broadcast_select_fusion.5 = bf16[1024,27,128]{2,1,0:T(8,128)(2,1)S(1)} fusion(bf16[1024,27,128]{2,1,0:T(8,128)(2,1)} %reshape.463, pred[1024,27]{1,0:T(8,128)(4,1)S(1)} %copy-done.14), kind=kLoop, calls=%fused_computation.29 | loop fusion | flops 3538944 | bytes 14183424 | tf_op jit(solution)/shard_map/jit(_take)/select_n | solution.py:66
  973.3 4.3 fusion.37
  977.7 15.7 %broadcast_select_fusion.4 = bf16[1024,27,128]{2,1,0:T(8,128)(2,1)S(1)} fusion(bf16[1024,27,128]{2,1,0:T(8,128)(2,1)} %reshape.467, pred[1024,27]{1,0:T(8,128)(4,1)S(1)} %copy-done.15), kind=kLoop, calls=%fused_computation.28 | loop fusion | flops 3538944 | bytes 14183424 | tf_op jit(solution)/shard_map/jit(_take)/select_n | solution.py:66
  993.5 4.3 fusion.34
  997.8 13.7 %broadcast_select_fusion.3 = bf16[1024,27,128]{2,1,0:T(8,128)(2,1)S(1)} fusion(bf16[1024,27,128]{2,1,0:T(8,128)(2,1)S(1)} %bitcast.389, pred[1024,27]{1,0:T(8,128)(4,1)S(1)} %copy-done.16), kind=kLoop, calls=%fused_computation.27 | loop fusion | flops 3538944 | bytes 14183424 | tf_op jit(solution)/shard_map/jit(_take)/select_n | solution.py:66
  1011.6 4.3 fusion.31
  1016.5 7.0 fusion.300
  1023.5 30.8 %all-gather.4.cloned.1.call-done = bf16[4096,256]{1,0:T(8,128)(2,1)} async-done(((bf16[1024,256]{1,0:T(8,128)(2,1)}), bf16[4096,256]{1,0:T(8,128)(2,1)}) %all-gather.4.cloned.1.call-update) | async-done | bytes 2097168 | tf_op jit(solution)/shard_map/all_gather | solution.py:204
  (336 shorter events, 155.6 us)
Async XLA Ops:
  6.5 387.6 %copy-start = (bf16[8,64,64]{2,1,0:T(8,128)(2,1)S(1)}, bf16[8,64,64]{2,1,0:T(8,128)(2,1)}, u32[]{:S(2)}) copy-start(bf16[8,64,64]{2,1,0:T(8,128)(2,1)} %param.26) | copy-start | bytes 196612
  6.5 29.9 %copy-start.11 = (bf16[4,64,64]{2,1,0:T(8,128)(2,1)S(1)}, bf16[4,64,64]{2,1,0:T(8,128)(2,1)}, u32[]{:S(2)}) copy-start(bf16[4,64,64]{2,1,0:T(8,128)(2,1)} %param.29) | copy-start | bytes 98308
  6.5 25.2 %copy-start.24 = (s32[1024,108]{0,1:T(8,128)S(1)}, s32[1024,108]{0,1:T(8,128)}, u32[]{:S(2)}) copy-start(s32[1024,108]{0,1:T(8,128)} %param.21) | copy-start | bytes 1327108
  6.5 30.7 %copy-start.9 = (bf16[2,64,64]{2,1,0:T(8,128)(2,1)S(1)}, bf16[2,64,64]{2,1,0:T(8,128)(2,1)}, u32[]{:S(2)}) copy-start(bf16[2,64,64]{2,1,0:T(8,128)(2,1)} %param.28) | copy-start | bytes 49156
  6.5 34.3 %copy-start.2 = (bf16[108,64,64]{0,2,1:T(8,128)(2,1)S(1)}, bf16[108,64,64]{0,2,1:T(8,128)(2,1)}, u32[]{:S(2)}) copy-start(bf16[108,64,64]{0,2,1:T(8,128)(2,1)} %param.27) | copy-start | bytes 2654212
  6.5 1047.8 %all-gather.4.cloned.1.call-start = ((), (), s32[]{:S(2)}) async-start(), calls=%async_computation | async-start | bytes 2621440 | tf_op jit(solution)/shard_map/all_gather | solution.py:204
  10.5 379.0 %collective-permute-start.2 = (bf16[768,128]{1,0:T(8,128)(2,1)}, bf16[768,128]{1,0:T(8,128)(2,1)}, u32[]{:S(2)}, u32[]{:S(2)}) collective-permute-start(bf16[768,128]{1,0:T(8,128)(2,1)} %copy.487), channel_id=1, source_target_pairs={{0,4},{4,8},{8,12},{12,16},{16,20},{20,24},{24,28},{28,32},{32,36}... | collective-permute-start | bytes 589832 | tf_op jit(solution)/shard_map/ppermute | solution.py:18
  13.3 376.3 %collective-permute-start.3 = (bf16[768,128]{1,0:T(8,128)(2,1)}, bf16[768,128]{1,0:T(8,128)(2,1)}, u32[]{:S(2)}, u32[]{:S(2)}) collective-permute-start(bf16[768,128]{1,0:T(8,128)(2,1)} %copy.488), channel_id=1, source_target_pairs={{4,0},{8,4},{12,8},{16,12},{20,16},{24,20},{28,24},{32,28},{36,32}... | collective-permute-start | bytes 589832 | tf_op jit(solution)/shard_map/ppermute | solution.py:20
  15.3 89.3 %collective-permute-start = (bf16[2,64,256]{2,1,0:T(8,128)(2,1)}, bf16[2,64,256]{2,1,0:T(8,128)(2,1)}, u32[]{:S(2)}, u32[]{:S(2)}) collective-permute-start(bf16[2,64,256]{2,1,0:T(8,128)(2,1)} %get-tuple-element.6), channel_id=1, source_target_pairs={{0,4},{4,8},{8,12},{12,16},{16,20},{20,24},{24,28},{28,32},{32,36}... | collective-permute-start | bytes 196616 | tf_op jit(solution)/shard_map/ppermute | solution.py:18
  20.1 84.4 %collective-permute-start.1 = (bf16[2,64,256]{2,1,0:T(8,128)(2,1)}, bf16[2,64,256]{2,1,0:T(8,128)(2,1)}, u32[]{:S(2)}, u32[]{:S(2)}) collective-permute-start(bf16[2,64,256]{2,1,0:T(8,128)(2,1)} %get-tuple-element.8), channel_id=1, source_target_pairs={{4,0},{8,4},{12,8},{16,12},{20,16},{24,20},{28,24},{32,28},{36,32}... | collective-permute-start | bytes 196616 | tf_op jit(solution)/shard_map/ppermute | solution.py:20
  64.0 19.5 %copy-start.35 = (s32[128,27]{0,1:T(8,128)S(1)}, s32[128,27]{0,1:T(8,128)}, u32[]{:S(2)}) copy-start(s32[128,27]{0,1:T(8,128)} %get-tuple-element.37) | copy-start | bytes 41476
  64.0 20.4 %copy-start.41 = (pred[128,27]{0,1:T(8,128)(4,1)S(1)}, pred[128,27]{0,1:T(8,128)(4,1)}, u32[]{:S(2)}) copy-start(pred[128,27]{0,1:T(8,128)(4,1)} %get-tuple-element.33) | copy-start | bytes 10372
  64.0 25.9 %copy-start.23 = (s32[1024,27]{0,1:T(8,128)S(1)}, s32[1024,27]{0,1:T(8,128)}, u32[]{:S(2)}) copy-start(s32[1024,27]{0,1:T(8,128)} %get-tuple-element.21) | copy-start | bytes 331780
  64.0 27.3 %copy-start.22 = (s32[1024,27]{0,1:T(8,128)S(1)}, s32[1024,27]{0,1:T(8,128)}, u32[]{:S(2)}) copy-start(s32[1024,27]{0,1:T(8,128)} %get-tuple-element.20) | copy-start | bytes 331780
  67.5 26.1 %copy-start.21 = (s32[1024,27]{0,1:T(8,128)S(1)}, s32[1024,27]{0,1:T(8,128)}, u32[]{:S(2)}) copy-start(s32[1024,27]{0,1:T(8,128)} %get-tuple-element.19) | copy-start | bytes 331780
  73.2 26.3 %copy-start.29 = (s32[1024,9]{0,1:T(8,128)S(1)}, s32[1024,9]{0,1:T(8,128)}, u32[]{:S(2)}) copy-start(s32[1024,9]{0,1:T(8,128)} %get-tuple-element.30) | copy-start | bytes 110596
  77.4 24.3 %copy-start.28 = (s32[1024,9]{0,1:T(8,128)S(1)}, s32[1024,9]{0,1:T(8,128)}, u32[]{:S(2)}) copy-start(s32[1024,9]{0,1:T(8,128)} %get-tuple-element.28) | copy-start | bytes 110596
  256.4 71.8 %copy-start.18 = (pred[1024,9]{1,0:T(8,128)(4,1)S(1)}, pred[1024,9]{1,0:T(8,128)(4,1)}, u32[]{:S(2)}) copy-start(pred[1024,9]{1,0:T(8,128)(4,1)} %copy.482) | copy-start | bytes 27652
  328.2 22.5 %slice-start.3 = ((s8[9437184]{0:T(1024)(128)(4,1)}), s8[4194304]{0:T(1024)(128)(4,1)S(1)}, s32[]{:S(2)}) async-start(s8[9437184]{0:T(1024)(128)(4,1)} %bitcast.384), calls=%async_computation.4 | async-start | bytes 8388608
  328.2 22.5 %slice-start.4 = ((s8[9437184]{0:T(1024)(128)(4,1)}), s8[4194304]{0:T(1024)(128)(4,1)S(1)}, s32[]{:S(2)}) async-start(s8[9437184]{0:T(1024)(128)(4,1)} %bitcast.384), calls=%async_computation.5 | async-start | bytes 8388608
  346.7 20.7 %slice-start = ((s8[9437184]{0:T(1024)(128)(4,1)}), s8[4194304]{0:T(1024)(128)(4,1)S(1)}, s32[]{:S(2)}) async-start(s8[9437184]{0:T(1024)(128)(4,1)} %bitcast.381), calls=%async_computation.1 | async-start | bytes 8388608
  346.7 20.7 %slice-start.1 = ((s8[9437184]{0:T(1024)(128)(4,1)}), s8[1048576]{0:T(1024)(128)(4,1)S(1)}, s32[]{:S(2)}) async-start(s8[9437184]{0:T(1024)(128)(4,1)} %bitcast.381), calls=%async_computation.2 | async-start | bytes 2097152
  389.5 34.2 %copy-start.10 = (bf16[2,64,64]{2,1,0:T(8,128)(2,1)S(1)}, bf16[2,64,64]{2,1,0:T(8,128)(2,1)}, u32[]{:S(2)}) copy-start(bf16[2,64,64]{2,1,0:T(8,128)(2,1)} %param.28) | copy-start | bytes 49156
  389.5 35.2 %copy-start.12 = (bf16[4,64,64]{2,1,0:T(8,128)(2,1)S(1)}, bf16[4,64,64]{2,1,0:T(8,128)(2,1)}, u32[]{:S(2)}) copy-start(bf16[4,64,64]{2,1,0:T(8,128)(2,1)} %param.29) | copy-start | bytes 98308
  389.5 47.4 %copy-start.37 = (s32[1024]{0:T(1024)S(1)}, s32[1024]{0:T(1024)}, u32[]{:S(2)}) copy-start(s32[1024]{0:T(1024)} %pad_clamp_fusion.7) | copy-start | bytes 12292
  389.5 49.0 %copy-start.38 = (s32[1024]{0:T(1024)S(1)}, s32[1024]{0:T(1024)}, u32[]{:S(2)}) copy-start(s32[1024]{0:T(1024)} %pad_clamp_fusion.6) | copy-start | bytes 12292
  389.6 51.2 %copy-start.39 = (s32[1024]{0:T(1024)S(1)}, s32[1024]{0:T(1024)}, u32[]{:S(2)}) copy-start(s32[1024]{0:T(1024)} %pad_clamp_fusion.5) | copy-start | bytes 12292
  394.7 54.3 %copy-start.6 = (bf16[27,128,128]{2,1,0:T(8,128)(2,1)S(1)}, bf16[27,128,128]{2,1,0:T(8,128)(2,1)}, u32[]{:S(2)}) copy-start(bf16[27,128,128]{2,1,0:T(8,128)(2,1)} %reshape.268) | copy-start | bytes 2654212
  973.3 24.5 %slice-start.6 = ((s8[8388608]{0:T(1024)(128)(4,1)}), s8[4194304]{0:T(1024)(128)(4,1)S(1)}, s32[]{:S(2)}) async-start(s8[8388608]{0:T(1024)(128)(4,1)} %bitcast.388), calls=%async_computation.7 | async-start | bytes 8388608
  977.7 20.1 %slice-start.7 = ((s8[8388608]{0:T(1024)(128)(4,1)}), s8[4194304]{0:T(1024)(128)(4,1)S(1)}, s32[]{:S(2)}) async-start(s8[8388608]{0:T(1024)(128)(4,1)} %bitcast.388), calls=%async_computation.8 | async-start | bytes 8388608
  1016.5 40.1 %copy-start.3 = (f32[2,1024,256]{2,1,0:T(8,128)S(1)}, f32[2,1024,256]{2,1,0:T(8,128)}, u32[]{:S(2)}) copy-start(f32[2,1024,256]{2,1,0:T(8,128)} %param.19) | copy-start | bytes 6291460
  1016.5 43.4 %copy-start.1 = (bf16[8,64,64]{2,1,0:T(8,128)(2,1)S(1)}, bf16[8,64,64]{2,1,0:T(8,128)(2,1)}, u32[]{:S(2)}) copy-start(bf16[8,64,64]{2,1,0:T(8,128)(2,1)} %param.26) | copy-start | bytes 196612
  (31 other events, 372.2 us)
Sparse Core Ops, SparseCore 0:
  1023.6 30.6 all-gather.3
